TPU v7x, 512 devices: a whole 4x4x16 slice. The times are simulated.
512 devices in a mesh: draw: 32 (over x_hi, z), img: 16 (over y, x_lo, core).
Axes of the slice: x: 4 (x_hi: 2, x_lo: 2; x = x_hi * 2 + x_lo), y: 4, z: 16, core: 2. Of those that a mesh axis runs over, the one named last changes fastest.
Arguments:
- features: bfloat16 [16, 32, 256, 1024], P('img', 'draw'), may hold values from -8 to 8
- cotangent: bfloat16 [16, 32, 256, 640], P('img', 'draw'), may hold values from -8 to 8
- time_index: int32 [16, 32], P('img', 'draw'), may hold values from 0 to 999, as said below
- mod_table: bfloat16 [1000, 1024], replicated, may hold values from -1.5 to 1.5
- weight: bfloat16 [1024, 640], replicated, may hold values from -0.1875 to 0.1875
Outputs:
- clipped_sum: float32 [1024, 640], P(('draw', 'img'))
- grad_input: bfloat16 [16, 32, 256, 1024], P('img', 'draw')
Inputs may be any that keep to these rules, and one draw needn't show every extreme that they name: `time_index`: draw k's timestep lies in the k-th of 32 strata: from k * 1000 // 32 to k * 1000 // 32 + 1000 // 32 - 1, except that the last draw's stratum runs on to 999.
All inputs are finite; a program needn't handle non-finite values.
Results may differ from a plain program's by a relative error of at most 0.0075.
Values may be sent and summed in bfloat16 or wider, within the bound.
A program may use at most 64 MiB of HBM per device.

v0:
```python
import math

import jax
import jax.numpy as jnp
from jax import lax
from jax.sharding import PartitionSpec as P


def local(features, cotangent, time_index, mod_table, weight):
    pixels = features.shape[2]
    in_width = features.shape[3]
    out_width = cotangent.shape[3]
    table_rows = mod_table.shape[0]
    draw_count = lax.axis_size("draw")
    feat_rows = features.reshape(pixels, in_width)
    one_hot = (lax.broadcasted_iota(jnp.int32, (1, table_rows), 1) == time_index).astype(
        jnp.bfloat16
    )
    modulation = jnp.dot(one_hot, mod_table, preferred_element_type=jnp.float32)
    gain = 1.0 + modulation
    pre_act = feat_rows.astype(jnp.float32) * gain
    acts = jax.nn.silu(pre_act).astype(jnp.bfloat16)
    loss_scale = 1.0 + 2.0 * time_index.astype(jnp.float32) / (table_rows - 1)
    weighted = (cotangent.reshape(pixels, out_width).astype(jnp.float32) * loss_scale).astype(
        jnp.bfloat16
    )
    back = lax.dot_general(
        weighted, weight, (((1,), (1,)), ((), ())), preferred_element_type=jnp.float32
    )
    gate_sig = jax.nn.sigmoid(pre_act)
    grad_input = (back * gate_sig * (1.0 + pre_act * (1.0 - gate_sig)) * gain).astype(jnp.bfloat16)
    grad_input = grad_input.reshape(features.shape)
    clip_bound = 0.3 * math.sqrt(in_width * out_width)
    partial_grad = lax.dot_general(
        acts, weighted, (((0,), (0,)), ((), ())), preferred_element_type=jnp.float32
    )
    image_grad = lax.psum(partial_grad, "draw") / draw_count
    norm_sq = jnp.sum(image_grad * image_grad)
    clip = jnp.minimum(1.0, clip_bound / jnp.sqrt(norm_sq + 1e-06))
    rows_draw = in_width // draw_count
    block = (
        lax.dynamic_slice_in_dim(image_grad, lax.axis_index("draw") * rows_draw, rows_draw, 0)
        * clip
    )
    clipped_sum = lax.psum_scatter(block, "img", scatter_dimension=0, tiled=True)
    return (clipped_sum, grad_input)


def solution(mesh):
    in_specs = (
        P("img", "draw", None, None),
        P("img", "draw", None, None),
        P("img", "draw"),
        P(),
        P(),
    )
    out_specs = (P(("draw", "img"), None), P("img", "draw", None, None))
    return jax.shard_map(local, mesh=mesh, in_specs=in_specs, out_specs=out_specs, check_vma=False)
```

profile of v0, /device:TPU:1, one launch (start us, length us, event | category | flops | bytes accessed | tf_op | source)
XLA Modules:
  0.0 457.4 jit_solution(7136724578651276840)
XLA Ops:
  7.2 0.0 copy-start
  7.2 0.0 all-reduce.4.cloned.1.call-start
  8.0 0.7 copy-done
  8.8 0.4 fusion.26
  9.2 3.5 fusion.18
  12.7 0.0 all-reduce.4.cloned.1.call-update
  12.7 0.0 all-reduce.6.cloned.1.call-start
  12.7 0.0 copy-start.1
  12.7 292.7 %all-reduce.4.cloned.1.call-done = f32[1024,640]{1,0:T(8,128)} async-done(((f32[1024,640]{1,0:T(8,128)}), f32[1024,640]{1,0:T(8,128)}) %all-reduce.4.cloned.1.call-update) | async-done | bytes 2621456 | tf_op jit(solution)/shard_map/psum | solution.py:37
  305.5 4.5 multiply_reduce_fusion
  310.7 1.5 dynamic-slice_multiply_fusion
  312.2 0.0 all-reduce.6.cloned.1.call-update
  312.2 0.0 copy-done.1
  312.2 2.7 fusion.5
  314.9 1.3 dynamic-slice
  316.8 132.4 %all-reduce.6.cloned.1.call-done = f32[32,640]{1,0:T(8,128)} async-done(((f32[32,640]{1,0:T(8,128)}), f32[32,640]{1,0:T(8,128)}) %all-reduce.6.cloned.1.call-update) | async-done | bytes 81936
  449.2 1.3 constant_dynamic-slice_fusion
  (3 shorter events, 0.0 us)
Async XLA Ops:
  7.2 1.6 copy-start
  7.2 298.3 %all-reduce.4.cloned.1.call-start = ((), (), s32[]{:S(2)}) async-start(), calls=%async_computation | async-start | bytes 5242880 | tf_op jit(solution)/shard_map/psum | solution.py:37
  12.7 436.6 %all-reduce.6.cloned.1.call-start = ((), (), s32[]{:S(2)}) async-start(), calls=%async_computation.1 | async-start | bytes 163840
  12.7 299.5 %copy-start.1 = (bf16[1024,640]{1,0:T(8,128)(2,1)S(1)}, bf16[1024,640]{1,0:T(8,128)(2,1)}, u32[]{:S(2)}) copy-start(bf16[1024,640]{1,0:T(8,128)(2,1)} %param.9) | copy-start | bytes 3932164
Sparse Core Ops, SparseCore 0:
  12.8 292.6 all-reduce.3
  312.3 136.8 all-reduce.5
where the time goes:
time: 458 us; the launch traced here: 457 us
  waiting for transfers between devices  425 us (93%)
  between operations  16.2 us (4%)
  matrix products  6.58 us (1%)
  other arithmetic  6.01 us (1%)
    psum x1, waiting for transfers between devices, local(): image_grad = lax.psum(partial_grad, 'draw') / draw_count  293 us
    unnamed x3, waiting for transfers between devices  132 us
  transfers between devices with their start and end apart: 2, of which 2 were waited for; matrix products, arithmetic and copies ran while one was open for 1% of the time, Pallas kernels for 0%

commit v1 on v0

v1 whole, which is shorter than its diff:
```python
import functools
import math

import jax
import jax.numpy as jnp
from jax import lax
from jax.experimental import pallas as pl
from jax.experimental.pallas import tpu as pltpu
from jax.sharding import PartitionSpec as P

MESH = pl.DeviceIdType.MESH
F32 = jnp.float32
BF16 = jnp.bfloat16
LANES = 128


def sigmoid(v):
    return 1.0 / (1.0 + jnp.exp(-v))


def kernel(
    draws, images, table_rows, window,
    feat_hbm, cot_hbm, time_hbm, table_hbm, weight_hbm,
    sum_ref, gi_hbm,
    feat, cot, when, rows, weight, gain, weighted, grad, gi,
    send, recv, cross_out, cross_in, norm_out, norm_in, part_out, part_in,
    load_sem, store_sem, send_sem, recv_sem, cross_sem, norm_sem, norm_recv, part_sem, part_recv,
):
    pixels, in_width = feat.shape
    ring = draws // 2
    half_rows = in_width // 2
    piece = in_width // draws
    each = piece // images
    k = lax.axis_index("draw")
    image = lax.axis_index("img")
    high = lax.div(k, ring)
    z = lax.rem(k, ring)

    def at_z(offset):
        return high * ring + lax.rem(z + offset + ring, ring)

    first_row = lax.div(k * table_rows, draws)
    first_block = jnp.minimum(lax.div(first_row, 8), table_rows // 8 - window)
    loads = [
        pltpu.make_async_copy(time_hbm, when, load_sem.at[0]),
        pltpu.make_async_copy(table_hbm.at[pl.ds(first_block, window)], rows, load_sem.at[1]),
        pltpu.make_async_copy(cot_hbm.at[0, 0], cot, load_sem.at[2]),
        pltpu.make_async_copy(feat_hbm.at[0, 0], feat, load_sem.at[3]),
        pltpu.make_async_copy(weight_hbm, weight, load_sem.at[4]),
    ]
    for load in loads:
        load.start()

    barrier = pltpu.get_barrier_semaphore()

    def greet_draw(o, _):
        pl.semaphore_signal(
            barrier, inc=1, device_id={"draw": lax.rem(k + o, draws)}, device_id_type=MESH
        )
        return 0

    def greet_image(o, _):
        pl.semaphore_signal(
            barrier, inc=1, device_id={"img": lax.rem(image + o, images)}, device_id_type=MESH
        )
        return 0

    lax.fori_loop(1, draws, greet_draw, 0)
    lax.fori_loop(1, images, greet_image, 0)

    for load in loads[:3]:
        load.wait()
    step = when[...]
    index = (
        lax.broadcasted_iota(jnp.int32, (window, 8, 1), 0) * 8
        + lax.broadcasted_iota(jnp.int32, (window, 8, 1), 1)
        + first_block * 8
    )
    chosen = jnp.where(index == step.reshape(1, 1, 1), rows[...].astype(F32), 0.0)
    gain[...] = 1.0 + jnp.sum(jnp.sum(chosen, axis=0), axis=0, keepdims=True)
    loss_scale = 1.0 + 2.0 * step.astype(F32) / (table_rows - 1)
    weighted[...] = (cot[...].astype(F32) * loss_scale).astype(BF16)
    loads[3].wait()

    for block in range(in_width // LANES):
        at = pl.ds(block * LANES, LANES)
        pre_act = feat[:, at].astype(F32) * gain[:, at]
        acts = (pre_act * sigmoid(pre_act)).astype(BF16)
        grad[at, :] = lax.dot_general(
            acts, weighted[...], (((0,), (0,)), ((), ())), preferred_element_type=F32
        )

    pl.semaphore_wait(barrier, draws - 1 + images - 1)

    streams = []
    for half in range(2):
        for way in range(2):
            hops = ring // 2 if half == way else ring // 2 - 1
            streams.append((half, way, hops))

    def ring_copy(half, way, left):
        return pltpu.make_async_remote_copy(
            src_ref=send.at[half, way, left],
            dst_ref=recv.at[half, way, left],
            send_sem=send_sem.at[half, way, left],
            recv_sem=recv_sem.at[half, way, left],
            device_id={"draw": at_z(1 if way == 0 else -1)},
            device_id_type=MESH,
        )

    def own(half, offset):
        start = half * half_rows + lax.rem(z + offset + ring, ring) * piece
        return grad[pl.ds(pl.multiple_of(start, piece), piece), :]

    def grad_input_block(block):
        at = pl.ds(block * LANES, LANES)
        back = lax.dot_general(
            weighted[...], weight[at, :], (((1,), (1,)), ((), ())), preferred_element_type=F32
        )
        scale = gain[:, at]
        pre_act = feat[:, at].astype(F32) * scale
        gate = sigmoid(pre_act)
        gi[:, at] = (back * gate * (1.0 + pre_act * (1.0 - gate)) * scale).astype(BF16)

    blocks = in_width // LANES
    steps = ring // 2
    done = 0
    for j in range(steps):
        for half, way, hops in streams:
            if j >= hops:
                continue
            left = hops - 1 - j
            term = own(half, (hops - j) if way == 0 else -(hops - j))
            if j > 0:
                ring_copy(half, way, left + 1).wait_recv()
                term = term + recv[half, way, left + 1].astype(F32)
            send[half, way, left] = term.astype(BF16)
            ring_copy(half, way, left).start()
        if j == 0:
            loads[4].wait()
        target = blocks * (j + 1) // steps
        while done < target:
            grad_input_block(done)
            done += 1
    store = pltpu.make_async_copy(gi, gi_hbm.at[0, 0], store_sem)
    store.start()

    for half in range(2):
        for way in range(2):
            ring_copy(half, way, 0).wait_recv()

    def whole(half):
        return own(half, 0) + recv[half, 0, 0].astype(F32) + recv[half, 1, 0].astype(F32)

    cross_out[...] = whole(1 - high).astype(BF16)
    cross = pltpu.make_async_remote_copy(
        src_ref=cross_out,
        dst_ref=cross_in,
        send_sem=cross_sem.at[0],
        recv_sem=cross_sem.at[1],
        device_id={"draw": (1 - high) * ring + z},
        device_id_type=MESH,
    )
    cross.start()
    mine = whole(high)
    cross.wait_recv()
    mine = (mine + cross_in[...].astype(F32)) * (1.0 / draws)

    square = mine * mine
    tile = square[:, 0:LANES]
    for c in range(1, square.shape[1] // LANES):
        tile = tile + square[:, c * LANES : (c + 1) * LANES]
    tile = jnp.sum(tile.reshape(piece // 8, 8, LANES), axis=0)
    norm_out[...] = tile

    def norm_copy(o):
        return pltpu.make_async_remote_copy(
            src_ref=norm_out,
            dst_ref=norm_in.at[o - 1],
            send_sem=norm_sem.at[o - 1],
            recv_sem=norm_recv.at[o - 1],
            device_id={"draw": lax.rem(k + o, draws)},
            device_id_type=MESH,
        )

    def norm_start(o, _):
        norm_copy(o).start()
        return 0

    def norm_wait(o, _):
        norm_copy(o).wait_recv()
        return 0

    lax.fori_loop(1, draws, norm_start, 0)
    lax.fori_loop(1, draws, norm_wait, 0)
    total = jnp.sum(norm_in[...], axis=0) + tile
    norm_sq = jnp.sum(jnp.sum(total, axis=0, keepdims=True), axis=1, keepdims=True)
    bound = 0.3 * math.sqrt(in_width * cot.shape[1])
    clip = jnp.minimum(1.0, bound / jnp.sqrt(norm_sq + 1e-06))
    mine = mine * clip

    for j in range(images):
        part_out[j] = mine[j * each : (j + 1) * each, :]

    def part_copy(o):
        to = lax.rem(image + o, images)
        return pltpu.make_async_remote_copy(
            src_ref=part_out.at[to],
            dst_ref=part_in.at[o],
            send_sem=part_sem.at[o],
            recv_sem=part_recv.at[o],
            device_id={"img": to},
            device_id_type=MESH,
        )

    def part_start(o, _):
        part_copy(o).start()
        return 0

    def part_wait(o, _):
        part_copy(o).wait_recv()
        return 0

    lax.fori_loop(1, images, part_start, 0)
    part_in[0] = part_out[image]
    lax.fori_loop(1, images, part_wait, 0)
    sum_ref[...] = jnp.sum(part_in[...], axis=0)

    def norm_sent(o, _):
        norm_copy(o).wait_send()
        return 0

    def part_sent(o, _):
        part_copy(o).wait_send()
        return 0

    for half, way, hops in streams:
        for left in range(hops):
            ring_copy(half, way, left).wait_send()
    cross.wait_send()
    lax.fori_loop(1, draws, norm_sent, 0)
    lax.fori_loop(1, images, part_sent, 0)
    store.wait()


def local(draws, images, features, cotangent, time_index, mod_table, weight):
    pixels, in_width = features.shape[2:]
    out_width = cotangent.shape[3]
    table_rows = mod_table.shape[0]
    stratum = table_rows - (draws - 1) * table_rows // draws
    window = (stratum + 14) // 8
    piece = in_width // draws
    each = piece // images
    hops = draws // 4
    dma = pltpu.SemaphoreType.DMA
    return pl.pallas_call(
        functools.partial(kernel, draws, images, table_rows, window),
        out_shape=(
            jax.ShapeDtypeStruct((each, out_width), F32),
            jax.ShapeDtypeStruct(features.shape, BF16),
        ),
        in_specs=[pl.BlockSpec(memory_space=pl.ANY)] * 5,
        out_specs=(
            pl.BlockSpec(memory_space=pltpu.VMEM),
            pl.BlockSpec(memory_space=pl.ANY),
        ),
        scratch_shapes=[
            pltpu.VMEM((pixels, in_width), BF16),
            pltpu.VMEM((pixels, out_width), BF16),
            pltpu.VMEM((1, 1), jnp.int32),
            pltpu.VMEM((window, 8, in_width), BF16),
            pltpu.VMEM((in_width, out_width), BF16),
            pltpu.VMEM((1, in_width), F32),
            pltpu.VMEM((pixels, out_width), BF16),
            pltpu.VMEM((in_width, out_width), F32),
            pltpu.VMEM((pixels, in_width), BF16),
            pltpu.VMEM((2, 2, hops, piece, out_width), BF16),
            pltpu.VMEM((2, 2, hops, piece, out_width), BF16),
            pltpu.VMEM((piece, out_width), BF16),
            pltpu.VMEM((piece, out_width), BF16),
            pltpu.VMEM((8, LANES), F32),
            pltpu.VMEM((draws - 1, 8, LANES), F32),
            pltpu.VMEM((images, each, out_width), F32),
            pltpu.VMEM((images, each, out_width), F32),
            dma((5,)),
            dma,
            dma((2, 2, hops)),
            dma((2, 2, hops)),
            dma((2,)),
            dma((draws - 1,)),
            dma((draws - 1,)),
            dma((images,)),
            dma((images,)),
        ],
        compiler_params=pltpu.CompilerParams(
            collective_id=0, has_side_effects=True, vmem_limit_bytes=48 * 2**20
        ),
        cost_estimate=pl.CostEstimate(
            flops=4 * pixels * in_width * out_width,
            bytes_accessed=2 * (2 * pixels * in_width + pixels * out_width + in_width * out_width),
            transcendentals=2 * pixels * in_width,
        ),
    )(
        features,
        cotangent,
        time_index,
        mod_table.reshape(table_rows // 8, 8, in_width),
        weight,
    )


def solution(mesh):
    in_specs = (
        P("img", "draw", None, None),
        P("img", "draw", None, None),
        P("img", "draw"),
        P(),
        P(),
    )
    out_specs = (P(("draw", "img"), None), P("img", "draw", None, None))
    body = functools.partial(local, mesh.shape["draw"], mesh.shape["img"])
    return jax.shard_map(body, mesh=mesh, in_specs=in_specs, out_specs=out_specs, check_vma=False)
```

time: 458 us -> 74.2 us (0.16)
  waiting for transfers between devices: 425 us -> 0 us
  Pallas kernels: 0 us -> 66.3 us
  between operations: 16.2 us -> 1.3 us
  matrix products: 6.58 us -> 0 us
  other arithmetic: 6.01 us -> 0 us
    psum x1 -> x0, waiting for transfers between devices: 293 us -> none  [local(): image_grad = lax.psum(partial_grad, 'draw') / draw_count]
    unnamed x3 -> x0, waiting for transfers between devices: 132 us -> none
    pallas_call x0 -> x1, Pallas kernels: none -> 66.3 us  [local(): pl.pallas_call(functools.partial(kernel, draws, images, table_rows, windo...]
    dot_general x3 -> x0, matrix products: 6.58 us -> none  [the longest x1 3.45 us: local(): lax.dot_general(acts, weighted, (((0,), (0,)), ((), ())), preferred_eleme...]
  transfers between devices with their start and end apart: 2 -> 0, of which waited for: 2 -> 0; matrix products, arithmetic and copies ran while one was open for 1% -> 0% of each run, Pallas kernels for 0% -> 0%
where the time goes in v1:
time: 74.2 us; the launch traced here: 73.9 us
  Pallas kernels  66.3 us (89%)
  local copies, waits for them, and re-layouts  6.28 us (8%)
  between operations  1.3 us (2%)
    pallas_call x1, Pallas kernels, local(): pl.pallas_call(functools.partial(kernel, draws, images, table_rows, windo...  66.3 us
    unnamed x10, local copies, waits for them, and re-layouts  6.28 us

profile of v1, /device:TPU:1, one launch (start us, length us, event | category | flops | bytes accessed | tf_op | source)
XLA Modules:
  0.0 73.9 jit_solution(4678388043880495406)
XLA Ops:
  1.3 0.0 copy-start
  1.3 1.6 %copy-done = bf16[1000,1024]{1,0:T(8,128)(2,1)S(1)} copy-done((bf16[1000,1024]{1,0:T(8,128)(2,1)S(1)}, bf16[1000,1024]{1,0:T(8,128)(2,1)}, u32[]{:S(2)}) %copy-start) | copy-done | bytes 2048024
  2.9 0.0 copy-start.1
  2.9 1.3 %copy-done.1 = bf16[1024,640]{1,0:T(8,128)(2,1)S(1)} copy-done((bf16[1024,640]{1,0:T(8,128)(2,1)S(1)}, bf16[1024,640]{1,0:T(8,128)(2,1)}, u32[]{:S(2)}) %copy-start.1) | copy-done | bytes 1310744
  4.2 0.0 copy-start.2
  4.2 1.0 %copy-done.2 = bf16[1,1,256,1024]{3,2,1,0:T(8,128)(2,1)S(1)} copy-done((bf16[1,1,256,1024]{3,2,1,0:T(8,128)(2,1)S(1)}, bf16[1,1,256,1024]{3,2,1,0:T(8,128)(2,1)}, u32[]{:S(2)}) %copy-start.2) | copy-done | bytes 524312
  5.2 0.0 copy-start.3
  5.2 1.0 %copy-done.3 = bf16[1,1,256,640]{3,2,1,0:T(8,128)(2,1)S(1)} copy-done((bf16[1,1,256,640]{3,2,1,0:T(8,128)(2,1)S(1)}, bf16[1,1,256,640]{3,2,1,0:T(8,128)(2,1)}, u32[]{:S(2)}) %copy-start.3) | copy-done | bytes 327704
  6.2 66.3 %shard_map.68 = (f32[2,640]{1,0:T(2,128)S(1)}, bf16[1,1,256,1024]{3,2,1,0:T(8,128)(2,1)S(1)}) custom-call(bf16[1,1,256,1024]{3,2,1,0:T(8,128)(2,1)S(1)} %copy-done.2, bf16[1,1,256,640]{3,2,1,0:T(8,128)(2,1)S(1)} %copy-done.3, s32[1,1]{1,0:T(1,128)S(6)} %copy.9.time_hbm, bf16[125,8,1024]{2,1,0:T(8,128)(2,1)S(1)} %bitcast.1, bf16[1024,640]{1,0:T(8,128)(2,1)S(1)} %copy-done.1), custom_call_target="tpu_custom_call" | custom-call | flops 671088640 | bytes 2686976 | tf_op jit(solution)/shard_map/pallas_call | solution.py:256
  72.5 0.6 copy.10
  73.1 0.8 %copy.11 = bf16[1,1,256,1024]{3,2,1,0:T(8,128)(2,1)} copy(bf16[1,1,256,1024]{3,2,1,0:T(8,128)(2,1)S(1)} %get-tuple-element.5) | data formatting | bytes 1048576
Async XLA Ops:
  1.3 1.6 %copy-start = (bf16[1000,1024]{1,0:T(8,128)(2,1)S(1)}, bf16[1000,1024]{1,0:T(8,128)(2,1)}, u32[]{:S(2)}) copy-start(bf16[1000,1024]{1,0:T(8,128)(2,1)} %param.8) | copy-start | bytes 6144004
  2.9 1.3 %copy-start.1 = (bf16[1024,640]{1,0:T(8,128)(2,1)S(1)}, bf16[1024,640]{1,0:T(8,128)(2,1)}, u32[]{:S(2)}) copy-start(bf16[1024,640]{1,0:T(8,128)(2,1)} %weight_hbm.1) | copy-start | bytes 3932164
  4.2 1.0 %copy-start.2 = (bf16[1,1,256,1024]{3,2,1,0:T(8,128)(2,1)S(1)}, bf16[1,1,256,1024]{3,2,1,0:T(8,128)(2,1)}, u32[]{:S(2)}) copy-start(bf16[1,1,256,1024]{3,2,1,0:T(8,128)(2,1)} %feat_hbm.1) | copy-start | bytes 1572868
  5.2 1.0 %copy-start.3 = (bf16[1,1,256,640]{3,2,1,0:T(8,128)(2,1)S(1)}, bf16[1,1,256,640]{3,2,1,0:T(8,128)(2,1)}, u32[]{:S(2)}) copy-start(bf16[1,1,256,640]{3,2,1,0:T(8,128)(2,1)} %cot_hbm.1) | copy-start | bytes 983044

commit v2 on v1

v2 whole, which is shorter than its diff:
```python
import functools
import math

import jax
import jax.numpy as jnp
from jax import lax
from jax.experimental import pallas as pl
from jax.experimental.pallas import tpu as pltpu
from jax.sharding import PartitionSpec as P

MESH = pl.DeviceIdType.MESH
F32 = jnp.float32
BF16 = jnp.bfloat16
LANES = 128
CROSS_FIRST = 512
LAG = 1
PART = BF16
TREES = {
    8: {8: 7, 7: 6, 6: 5, 5: 0, 4: 3, 3: 2, 2: 1, 1: 0},
    7: {7: 6, 6: 5, 5: 0, 4: 3, 3: 2, 2: 1, 1: 0},
}


def sigmoid(v):
    return 1.0 / (1.0 + jnp.exp(-v))


def tree_levels(tree):
    level = {}
    for node in sorted(tree, reverse=True):
        level[node] = max([level[c] + 1 for c in tree if tree[c] == node], default=0)
    return level


def kernel(
    draws, images, table_rows, window,
    feat_hbm, cot_hbm, time_hbm, table_hbm, weight_hbm,
    sum_ref, gi_hbm,
    feat, cot, when, rows, weight, gain, weighted, grad, gi,
    first_out, first_in, xsend, xrecv, zsend, zrecv, cross_out, cross_in,
    norm_out, norm_in, part_out, part_in,
    load_sem, store_sem, first_send, first_recv, xsend_sem, xrecv_sem, zsend_sem, zrecv_sem,
    cross_sem, norm_sem, part_sem,
):
    in_width = feat.shape[1]
    out_width = cot.shape[1]
    ring = draws // 2
    half_rows = in_width // 2
    piece = in_width // draws
    each = piece // images
    first_cols = slice(0, CROSS_FIRST)
    late_cols = slice(CROSS_FIRST, out_width)
    k = lax.axis_index("draw")
    image = lax.axis_index("img")
    high = lax.div(k, ring)
    z = lax.rem(k, ring)

    def around(offset):
        return lax.rem(z + (offset + ring), ring)

    def at_z(offset):
        return {"draw": high * ring + around(offset)}

    partner = {"draw": (1 - high) * ring + z}

    first_row = lax.div(k * table_rows, draws)
    first_block = jnp.minimum(lax.div(first_row, 8), table_rows // 8 - window)
    loads = [
        pltpu.make_async_copy(time_hbm, when, load_sem.at[0]),
        pltpu.make_async_copy(table_hbm.at[pl.ds(first_block, window)], rows, load_sem.at[1]),
        pltpu.make_async_copy(cot_hbm.at[0, 0], cot, load_sem.at[2]),
        pltpu.make_async_copy(feat_hbm.at[0, 0], feat, load_sem.at[3]),
        pltpu.make_async_copy(weight_hbm, weight, load_sem.at[4]),
    ]
    for load in loads:
        load.start()

    trees = {ring // 2: TREES[ring // 2], ring // 2 - 1: TREES[ring // 2 - 1]}
    reach = sorted({node - tree[node] for tree in trees.values() for node in tree})
    barrier = pltpu.get_barrier_semaphore()
    for hop in reach:
        for offset in (hop, -hop):
            pl.semaphore_signal(barrier, inc=1, device_id=at_z(offset), device_id_type=MESH)
    pl.semaphore_signal(barrier, inc=1, device_id=partner, device_id_type=MESH)

    def greet_image(o, _):
        pl.semaphore_signal(
            barrier, inc=1, device_id={"img": lax.rem(image + o, images)}, device_id_type=MESH
        )
        return 0

    lax.fori_loop(1, images, greet_image, 0)

    for load in loads[:3]:
        load.wait()
    step = when[...]
    index = (
        lax.broadcasted_iota(jnp.int32, (window, 8, 1), 0) * 8
        + lax.broadcasted_iota(jnp.int32, (window, 8, 1), 1)
        + first_block * 8
    )
    chosen = jnp.where(index == step.reshape(1, 1, 1), rows[...].astype(F32), 0.0)
    gain[...] = 1.0 + jnp.sum(jnp.sum(chosen, axis=0), axis=0, keepdims=True)
    loss_scale = 1.0 + 2.0 * step.astype(F32) / (table_rows - 1)
    weighted[...] = (cot[...].astype(F32) * loss_scale).astype(BF16)
    loads[3].wait()

    for block in range(in_width // LANES):
        at = pl.ds(block * LANES, LANES)
        pre_act = feat[:, at].astype(F32) * gain[:, at]
        acts = (pre_act * sigmoid(pre_act)).astype(BF16)
        grad[at, :] = lax.dot_general(
            acts, weighted[...], (((0,), (0,)), ((), ())), preferred_element_type=F32
        )

    pl.semaphore_wait(barrier, 2 * len(reach) + images)

    def own(half, offset, cols):
        start = half * half_rows + around(offset) * piece
        return grad[pl.ds(pl.multiple_of(start, piece), piece), cols]

    def first_copy(n):
        return pltpu.make_async_remote_copy(
            src_ref=first_out.at[n],
            dst_ref=first_in.at[n],
            send_sem=first_send.at[n],
            recv_sem=first_recv.at[n],
            device_id=partner,
            device_id_type=MESH,
        )

    def first_start(n):
        first_out[n] = own(1 - high, n, first_cols).astype(BF16)
        first_copy(n).start()

    arrived = set()

    def first_own(offset):
        n = offset % ring
        if n not in arrived:
            arrived.add(n)
            first_copy(n).wait_recv()
        return own(high, offset, first_cols) + first_in[n].astype(F32)

    def zcopy(half, way, node, hop):
        return pltpu.make_async_remote_copy(
            src_ref=zsend.at[half, way, node - 1],
            dst_ref=zrecv.at[half, way, node - 1],
            send_sem=zsend_sem.at[half, way, node - 1],
            recv_sem=zrecv_sem.at[half, way, node - 1],
            device_id=at_z(hop if way == 0 else -hop),
            device_id_type=MESH,
        )

    def xcopy(way, node, hop):
        return pltpu.make_async_remote_copy(
            src_ref=xsend.at[way, node - 1],
            dst_ref=xrecv.at[way, node - 1],
            send_sem=xsend_sem.at[way, node - 1],
            recv_sem=xrecv_sem.at[way, node - 1],
            device_id=at_z(hop if way == 0 else -hop),
            device_id_type=MESH,
        )

    jobs = []
    for way in range(2):
        for half in range(2):
            tree = trees[ring // 2 if half == way else ring // 2 - 1]
            for node, level in tree_levels(tree).items():
                jobs.append((level, 0, -node, half, way, tree))
        tree = trees[ring // 2 if way == 0 else ring // 2 - 1]
        for node, level in tree_levels(tree).items() if CROSS_FIRST else ():
            jobs.append((level + LAG, 1, -node, 0, way, tree))
    jobs.sort(key=lambda job: job[:5])

    def children(tree, node):
        return [c for c in tree if tree[c] == node]

    def total(kind, half, way, tree, node, offset):
        if kind == 0:
            term = own(half, offset, late_cols)
            for c in children(tree, node):
                zcopy(half, way, c, c - node).wait_recv()
                term = term + zrecv[half, way, c - 1].astype(F32)
        else:
            term = first_own(offset)
            for c in children(tree, node):
                xcopy(way, c, c - node).wait_recv()
                term = term + xrecv[way, c - 1].astype(F32)
        return term

    def grad_input_block(block):
        at = pl.ds(block * LANES, LANES)
        back = lax.dot_general(
            weighted[...], weight[at, :], (((1,), (1,)), ((), ())), preferred_element_type=F32
        )
        scale = gain[:, at]
        pre_act = feat[:, at].astype(F32) * scale
        gate = sigmoid(pre_act)
        gi[:, at] = (back * gate * (1.0 + pre_act * (1.0 - gate)) * scale).astype(BF16)

    if CROSS_FIRST:
        order = []
        for level, kind, minus, half, way, tree in jobs:
            if kind == 1:
                n = (-minus if way == 0 else minus) % ring
                if n not in order:
                    order.append(n)
        order.append(0)
        for n in order:
            first_start(n)
    blocks = in_width // LANES
    done = 0
    sent = []
    last = jobs[-1][0]
    for at, (level, kind, minus, half, way, tree) in enumerate(jobs):
        node = -minus
        offset = node if way == 0 else -node
        hop = node - tree[node]
        term = total(kind, half, way, tree, node, offset).astype(BF16)
        if kind == 0:
            zsend[half, way, node - 1] = term
            copy = zcopy(half, way, node, hop)
        else:
            xsend[way, node - 1] = term
            copy = xcopy(way, node, hop)
        copy.start()
        sent.append(copy)
        if at + 1 == len(jobs) or jobs[at + 1][0] > level:
            target = blocks * (level + 1) // (last + 1)
            if done == 0 and target > 0:
                loads[4].wait()
            while done < target:
                grad_input_block(done)
                done += 1
    store = pltpu.make_async_copy(gi, gi_hbm.at[0, 0], store_sem)
    store.start()

    root8 = set(children(trees[ring // 2], 0))
    root7 = set(children(trees[ring // 2 - 1], 0))
    for half in range(2):
        for way in range(2):
            for c in sorted(root8 if half == way else root7, reverse=True):
                zcopy(half, way, c, c).wait_recv()
    shared = sorted(root8 & root7)

    def whole(half):
        value = own(half, 0, late_cols)
        for way in range(2):
            for c in shared:
                value = value + zrecv[half, way, c - 1].astype(F32)
        for c in sorted(root8 - root7):
            value = value + zrecv[half, half, c - 1].astype(F32)
        for c in sorted(root7 - root8):
            value = value + zrecv[half, 1 - half, c - 1].astype(F32)
        return value

    cross_out[...] = whole(1 - high).astype(BF16)
    cross = pltpu.make_async_remote_copy(
        src_ref=cross_out,
        dst_ref=cross_in,
        send_sem=cross_sem.at[0],
        recv_sem=cross_sem.at[1],
        device_id=partner,
        device_id_type=MESH,
    )
    cross.start()
    sent.append(cross)
    parts = []
    if CROSS_FIRST:
        value = first_own(0)
        for way in range(2):
            tree = trees[ring // 2 if way == 0 else ring // 2 - 1]
            for c in children(tree, 0):
                xcopy(way, c, c).wait_recv()
                value = value + xrecv[way, c - 1].astype(F32)
        parts.append(value)
        sent += [first_copy(n) for n in order]
    value = whole(high)
    cross.wait_recv()
    parts.append(value + cross_in[...].astype(F32))
    mine = jnp.concatenate(parts, axis=1) * (1.0 / draws)

    def finish():
        for copy in sent:
            copy.wait_send()
        store.wait()


    square = mine * mine
    tile = square[:, 0:LANES]
    for c in range(1, out_width // LANES):
        tile = tile + square[:, c * LANES : (c + 1) * LANES]
    norm_out[...] = jnp.sum(tile, axis=0, keepdims=True)

    def norm_start(o, _):
        pltpu.make_async_remote_copy(
            src_ref=norm_out,
            dst_ref=norm_in.at[o],
            send_sem=norm_sem.at[0],
            recv_sem=norm_sem.at[1],
            device_id={"draw": lax.rem(k + o, draws)},
            device_id_type=MESH,
        ).start()
        return 0

    lax.fori_loop(1, draws, norm_start, 0)
    norm_in[0] = norm_out[...]
    norm_all = norm_in.at[pl.ds(1, draws - 1)]
    pltpu.make_async_copy(norm_all, norm_all, norm_sem.at[1]).wait()
    norm_sq = jnp.sum(jnp.sum(norm_in[...], axis=0), axis=1, keepdims=True)
    bound = 0.3 * math.sqrt(in_width * out_width)
    clip = jnp.minimum(1.0, bound / jnp.sqrt(norm_sq + 1e-06))
    mine = mine * clip

    for j in range(images):
        part_out[j] = mine[j * each : (j + 1) * each, :].astype(part_out.dtype)

    def part_start(o, _):
        to = lax.rem(image + o, images)
        pltpu.make_async_remote_copy(
            src_ref=part_out.at[to],
            dst_ref=part_in.at[o],
            send_sem=part_sem.at[0],
            recv_sem=part_sem.at[1],
            device_id={"img": to},
            device_id_type=MESH,
        ).start()
        return 0

    lax.fori_loop(1, images, part_start, 0)
    part_in[0] = part_out[image]
    part_all = part_in.at[pl.ds(1, images - 1)]
    pltpu.make_async_copy(part_all, part_all, part_sem.at[1]).wait()
    sum_ref[...] = jnp.sum(part_in[...].astype(F32), axis=0)

    finish()
    pltpu.make_async_copy(norm_all, norm_all, norm_sem.at[0]).wait()
    pltpu.make_async_copy(part_all, part_all, part_sem.at[0]).wait()


def local(draws, images, features, cotangent, time_index, mod_table, weight):
    pixels, in_width = features.shape[2:]
    out_width = cotangent.shape[3]
    table_rows = mod_table.shape[0]
    stratum = table_rows - (draws - 1) * table_rows // draws
    window = (stratum + 14) // 8
    piece = in_width // draws
    each = piece // images
    hops = draws // 4
    first = CROSS_FIRST or LANES
    late = out_width - CROSS_FIRST
    dma = pltpu.SemaphoreType.DMA
    return pl.pallas_call(
        functools.partial(kernel, draws, images, table_rows, window),
        out_shape=(
            jax.ShapeDtypeStruct((each, out_width), F32),
            jax.ShapeDtypeStruct(features.shape, BF16),
        ),
        in_specs=[pl.BlockSpec(memory_space=pltpu.HBM)] * 5,
        out_specs=(
            pl.BlockSpec(memory_space=pltpu.VMEM),
            pl.BlockSpec(memory_space=pl.ANY),
        ),
        scratch_shapes=[
            pltpu.VMEM((pixels, in_width), BF16),
            pltpu.VMEM((pixels, out_width), BF16),
            pltpu.VMEM((1, 1), jnp.int32),
            pltpu.VMEM((window, 8, in_width), BF16),
            pltpu.VMEM((in_width, out_width), BF16),
            pltpu.VMEM((1, in_width), F32),
            pltpu.VMEM((pixels, out_width), BF16),
            pltpu.VMEM((in_width, out_width), F32),
            pltpu.VMEM((pixels, in_width), BF16),
            pltpu.VMEM((draws // 2, piece, first), BF16),
            pltpu.VMEM((draws // 2, piece, first), BF16),
            pltpu.VMEM((2, hops, piece, first), BF16),
            pltpu.VMEM((2, hops, piece, first), BF16),
            pltpu.VMEM((2, 2, hops, piece, late), BF16),
            pltpu.VMEM((2, 2, hops, piece, late), BF16),
            pltpu.VMEM((piece, late), BF16),
            pltpu.VMEM((piece, late), BF16),
            pltpu.VMEM((1, LANES), F32),
            pltpu.VMEM((draws, 1, LANES), F32),
            pltpu.VMEM((images, each, out_width), PART),
            pltpu.VMEM((images, each, out_width), PART),
            dma((5,)),
            dma,
            dma((draws // 2,)),
            dma((draws // 2,)),
            dma((2, hops)),
            dma((2, hops)),
            dma((2, 2, hops)),
            dma((2, 2, hops)),
            dma((2,)),
            dma((2,)),
            dma((2,)),
        ],
        compiler_params=pltpu.CompilerParams(
            collective_id=0, has_side_effects=True, vmem_limit_bytes=60 * 2**20
        ),
        cost_estimate=pl.CostEstimate(
            flops=4 * pixels * in_width * out_width,
            bytes_accessed=2 * (2 * pixels * in_width + pixels * out_width + in_width * out_width),
            transcendentals=2 * pixels * in_width,
        ),
    )(
        features,
        cotangent,
        time_index,
        mod_table.reshape(table_rows // 8, 8, in_width),
        weight,
    )


def solution(mesh):
    in_specs = (
        P("img", "draw", None, None),
        P("img", "draw", None, None),
        P("img", "draw"),
        P(),
        P(),
    )
    out_specs = (P(("draw", "img"), None), P("img", "draw", None, None))
    body = functools.partial(local, mesh.shape["draw"], mesh.shape["img"])
    return jax.shard_map(body, mesh=mesh, in_specs=in_specs, out_specs=out_specs, check_vma=False)
```

time: 74.2 us -> 56.2 us (0.76)
  Pallas kernels: 66.3 us -> 51.5 us
  local copies, waits for them, and re-layouts: 6.28 us -> 3.15 us
    pallas_call x1, Pallas kernels: 66.3 us -> 51.5 us  [local(): pl.pallas_call(functools.partial(kernel, draws, images, table_rows, windo...]
    unnamed x10 -> x2, local copies, waits for them, and re-layouts: 6.28 us -> 3.15 us
where the time goes in v2:
time: 56.2 us; the launch traced here: 55.9 us
  Pallas kernels  51.5 us (92%)
  local copies, waits for them, and re-layouts  3.15 us (6%)
  between operations  1.28 us (2%)
    pallas_call x1, Pallas kernels, local(): pl.pallas_call(functools.partial(kernel, draws, images, table_rows, windo...  51.5 us
    unnamed x2, local copies, waits for them, and re-layouts  3.15 us

profile of v2, /device:TPU:1, one launch (start us, length us, event | category | flops | bytes accessed | tf_op | source)
XLA Modules:
  0.0 55.9 jit_solution(2331080431431517057)
XLA Ops:
  1.3 51.5 %shard_map.68 = (f32[2,640]{1,0:T(2,128)}, bf16[1,1,256,1024]{3,2,1,0:T(8,128)(2,1)}) custom-call(bf16[1,1,256,1024]{3,2,1,0:T(8,128)(2,1)} %feat_hbm.1, bf16[1,1,256,640]{3,2,1,0:T(8,128)(2,1)} %cot_hbm.1, s32[1,1]{1,0:T(1,128)S(6)} %copy.9.time_hbm, bf16[125,8,1024]{2,1,0:T(8,128)(2,1)} %bitcast.1, bf16[1024,640]{1,0:T(8,128)(2,1)} %weight_hbm.1), custom_call_target="tpu_custom_call" | custom-call | flops 671088640 | bytes 2686976 | tf_op jit(solution)/shard_map/pallas_call | solution.py:354
  52.8 1.3 %copy.10 = f32[2,640]{1,0:T(2,128)} copy(f32[2,640]{1,0:T(2,128)} %get-tuple-element.4) | data formatting | bytes 10240
  54.1 1.9 %copy.11 = bf16[1,1,256,1024]{3,2,1,0:T(8,128)(2,1)} copy(bf16[1,1,256,1024]{3,2,1,0:T(8,128)(2,1)} %get-tuple-element.5) | data formatting | bytes 1048576

commit v3 on v2

v3 whole, which is shorter than its diff:
```python
import functools
import math

import jax
import jax.numpy as jnp
from jax import lax
from jax.experimental import pallas as pl
from jax.experimental.pallas import tpu as pltpu
from jax.sharding import PartitionSpec as P

MESH = pl.DeviceIdType.MESH
F32 = jnp.float32
BF16 = jnp.bfloat16
LANES = 128
LAG = 0
NEAR = {3: 2, 2: 1, 1: 0}
FAR = {8: 6, 7: 6, 6: 4, 5: 4, 4: 0}


def sigmoid(v):
    return 1.0 / (1.0 + jnp.exp(-v))


def tree_levels(tree):
    level = {}
    for node in sorted(tree, reverse=True):
        level[node] = max([level[c] + 1 for c in tree if tree[c] == node], default=0)
    return level


def kernel(
    draws, images, table_rows, window,
    feat_hbm, cot_hbm, time_hbm, table_hbm, weight_hbm,
    sum_ref, gi_ref,
    feat, cot, when, rows, weight, gain, weighted, grad,
    first_out, first_in, xsend, xrecv, zsend, zrecv, both, cross_out, cross_in,
    plane_out, plane_in, norm_out, norm_in, part_out, part_in,
    load_sem, first_send, first_recv, xsend_sem, xrecv_sem, zsend_sem, zrecv_sem,
    cross_sem, plane_sem, norm_sem, part_sem,
):
    in_width = feat.shape[1]
    out_width = cot.shape[1]
    ring = draws // 2
    half_rows = in_width // 2
    piece = in_width // draws
    each = piece // images
    k = lax.axis_index("draw")
    image = lax.axis_index("img")
    high = lax.div(k, ring)
    z = lax.rem(k, ring)

    def around(offset):
        return lax.rem(z + (offset + ring), ring)

    def at_z(offset):
        return {"draw": high * ring + around(offset)}

    partner = {"draw": (1 - high) * ring + z}

    first_row = lax.div(k * table_rows, draws)
    first_block = jnp.minimum(lax.div(first_row, 8), table_rows // 8 - window)
    loads = [
        pltpu.make_async_copy(time_hbm, when, load_sem.at[0]),
        pltpu.make_async_copy(table_hbm.at[pl.ds(first_block, window)], rows, load_sem.at[1]),
        pltpu.make_async_copy(cot_hbm.at[0, 0], cot, load_sem.at[2]),
        pltpu.make_async_copy(feat_hbm.at[0, 0], feat, load_sem.at[3]),
        pltpu.make_async_copy(weight_hbm, weight, load_sem.at[4]),
    ]
    for load in loads:
        load.start()

    near, far = (NEAR, NEAR), (FAR, {c: p for c, p in FAR.items() if c != ring // 2})
    reach = sorted({c - p for tree in (NEAR, FAR) for c, p in tree.items()})
    barrier = pltpu.get_barrier_semaphore()
    for hop in reach:
        for offset in (hop, -hop):
            pl.semaphore_signal(barrier, inc=1, device_id=at_z(offset), device_id_type=MESH)
    pl.semaphore_signal(barrier, inc=1, device_id=partner, device_id_type=MESH)

    def greet_image(o, _):
        pl.semaphore_signal(
            barrier, inc=1, device_id={"img": lax.rem(image + o, images)}, device_id_type=MESH
        )
        return 0

    lax.fori_loop(1, images, greet_image, 0)

    for load in loads[:3]:
        load.wait()
    step = when[...]
    index = (
        lax.broadcasted_iota(jnp.int32, (window, 8, 1), 0) * 8
        + lax.broadcasted_iota(jnp.int32, (window, 8, 1), 1)
        + first_block * 8
    )
    chosen = jnp.where(index == step.reshape(1, 1, 1), rows[...].astype(F32), 0.0)
    gain[...] = 1.0 + jnp.sum(jnp.sum(chosen, axis=0), axis=0, keepdims=True)
    loss_scale = 1.0 + 2.0 * step.astype(F32) / (table_rows - 1)
    weighted[...] = (cot[...].astype(F32) * loss_scale).astype(BF16)
    loads[3].wait()

    for block in range(in_width // LANES):
        at = pl.ds(block * LANES, LANES)
        pre_act = feat[:, at].astype(F32) * gain[:, at]
        acts = (pre_act * sigmoid(pre_act)).astype(BF16)
        grad[at, :] = lax.dot_general(
            acts, weighted[...], (((0,), (0,)), ((), ())), preferred_element_type=F32
        )

    pl.semaphore_wait(barrier, 2 * len(reach) + images)

    def own(half, offset):
        start = half * half_rows + around(offset) * piece
        return grad[pl.ds(pl.multiple_of(start, piece), piece), :]

    def first_copy(n):
        return pltpu.make_async_remote_copy(
            src_ref=first_out.at[n],
            dst_ref=first_in.at[n],
            send_sem=first_send.at[n],
            recv_sem=first_recv.at[n],
            device_id=partner,
            device_id_type=MESH,
        )

    def near_copy(half, way, node, hop):
        return pltpu.make_async_remote_copy(
            src_ref=zsend.at[half, way, node - 1],
            dst_ref=zrecv.at[half, way, node - 1],
            send_sem=zsend_sem.at[half, way, node - 1],
            recv_sem=zrecv_sem.at[half, way, node - 1],
            device_id=at_z(hop if way == 0 else -hop),
            device_id_type=MESH,
        )

    def far_copy(way, node, hop):
        return pltpu.make_async_remote_copy(
            src_ref=xsend.at[way, node - 1],
            dst_ref=xrecv.at[way, node - 1],
            send_sem=xsend_sem.at[way, node - 1],
            recv_sem=xrecv_sem.at[way, node - 1],
            device_id=at_z(hop if way == 0 else -hop),
            device_id_type=MESH,
        )

    def children(tree, node):
        return [c for c in tree if tree[c] == node]

    def near_sum(half, way, node, term):
        for c in children(near[way], node):
            near_copy(half, way, c, c - node).wait_recv()
            term = term + zrecv[half, way, c - 1].astype(F32)
        return term

    def far_sum(way, node, term):
        for c in children(far[way], node):
            far_copy(way, c, c - node).wait_recv()
            term = term + xrecv[way, c - 1].astype(F32)
        return term

    def grad_input_block(block):
        at = pl.ds(block * LANES, LANES)
        back = lax.dot_general(
            weighted[...], weight[at, :], (((1,), (1,)), ((), ())), preferred_element_type=F32
        )
        scale = gain[:, at]
        pre_act = feat[:, at].astype(F32) * scale
        gate = sigmoid(pre_act)
        gi_ref[0, 0, :, at] = (back * gate * (1.0 + pre_act * (1.0 - gate)) * scale).astype(BF16)

    jobs = []
    for way in range(2):
        for node, level in tree_levels(near[way]).items():
            jobs += [(level, 0, -node, half, way) for half in range(2)]
        for node, level in tree_levels(far[way]).items():
            jobs.append((level + LAG, 1, -node, 0, way))
    jobs.sort()
    sent = []
    for _, kind, minus, _, way in jobs:
        if kind == 1:
            offset = -minus if way == 0 else minus
            first_out[offset % ring] = own(1 - high, offset).astype(BF16)
            sent.append(first_copy(offset % ring))
            sent[-1].start()
    blocks = in_width // LANES
    done = 0
    last = jobs[-1][0]
    for at, (level, kind, minus, half, way) in enumerate(jobs):
        node = -minus
        offset = node if way == 0 else -node
        if kind == 0:
            term = near_sum(half, way, node, own(half, offset))
            zsend[half, way, node - 1] = term.astype(BF16)
            copy = near_copy(half, way, node, node - near[way][node])
        else:
            first_copy(offset % ring).wait_recv()
            term = own(high, offset) + first_in[offset % ring].astype(F32)
            xsend[way, node - 1] = far_sum(way, node, term).astype(BF16)
            copy = far_copy(way, node, node - far[way][node])
        copy.start()
        sent.append(copy)
        if at + 1 == len(jobs) or jobs[at + 1][0] > level:
            target = blocks * (level + 1) // (last + 1)
            if done == 0 and target > 0:
                loads[4].wait()
            while done < target:
                grad_input_block(done)
                done += 1

    for half in range(2):
        term = own(half, 0)
        for way in range(2):
            term = near_sum(half, way, 0, term)
        both[half] = term
    cross_out[...] = both[1 - high].astype(BF16)
    cross = pltpu.make_async_remote_copy(
        src_ref=cross_out,
        dst_ref=cross_in,
        send_sem=cross_sem.at[0],
        recv_sem=cross_sem.at[1],
        device_id=partner,
        device_id_type=MESH,
    )
    cross.start()
    sent.append(cross)
    mine = both[high]
    cross.wait_recv()
    mine = mine + cross_in[...].astype(F32)
    for way in range(2):
        mine = far_sum(way, 0, mine)
    mine = mine * (1.0 / draws)

    def finish():
        for copy in sent:
            copy.wait_send()


    square = mine * mine
    tile = square[:, 0:LANES]
    for c in range(1, out_width // LANES):
        tile = tile + square[:, c * LANES : (c + 1) * LANES]
    plane_out[...] = jnp.sum(tile, axis=0, keepdims=True)

    def plane_start(o, _):
        pltpu.make_async_remote_copy(
            src_ref=plane_out,
            dst_ref=plane_in.at[o],
            send_sem=plane_sem.at[0],
            recv_sem=plane_sem.at[1],
            device_id={"img": lax.rem(image + o, images)},
            device_id_type=MESH,
        ).start()
        return 0

    lax.fori_loop(1, images, plane_start, 0)
    for j in range(images):
        part_out[j] = mine[j * each : (j + 1) * each, :].astype(BF16)

    def part_start(o, _):
        to = lax.rem(image + o, images)
        pltpu.make_async_remote_copy(
            src_ref=part_out.at[to],
            dst_ref=part_in.at[o],
            send_sem=part_sem.at[0],
            recv_sem=part_sem.at[1],
            device_id={"img": to},
            device_id_type=MESH,
        ).start()
        return 0

    lax.fori_loop(1, images, part_start, 0)
    plane_in[0] = plane_out[...]
    part_in[0] = part_out[image]
    plane_all = plane_in.at[pl.ds(1, images - 1)]
    pltpu.make_async_copy(plane_all, plane_all, plane_sem.at[1]).wait()

    lane = lax.broadcasted_iota(jnp.int32, (images, 1, LANES), 2)
    slot = lax.broadcasted_iota(jnp.int32, (images, 1, LANES), 0)
    shares = jnp.sum(plane_in[...], axis=2, keepdims=True)
    norm_out[...] = jnp.sum(jnp.where(lane == slot, shares, 0.0), axis=0)

    def norm_start(o, _):
        pltpu.make_async_remote_copy(
            src_ref=norm_out,
            dst_ref=norm_in.at[o],
            send_sem=norm_sem.at[0],
            recv_sem=norm_sem.at[1],
            device_id={"draw": lax.rem(k + o, draws)},
            device_id_type=MESH,
        ).start()
        return 0

    lax.fori_loop(1, draws, norm_start, 0)
    norm_in[0] = norm_out[...]
    part_all = part_in.at[pl.ds(1, images - 1)]
    pltpu.make_async_copy(part_all, part_all, part_sem.at[1]).wait()
    finish()
    pltpu.make_async_copy(plane_all, plane_all, plane_sem.at[0]).wait()
    pltpu.make_async_copy(part_all, part_all, part_sem.at[0]).wait()
    norm_all = norm_in.at[pl.ds(1, draws - 1)]
    pltpu.make_async_copy(norm_all, norm_all, norm_sem.at[1]).wait()
    norm_sq = jnp.sum(norm_in[...], axis=0)
    bound = 0.3 * math.sqrt(in_width * out_width)
    clip = jnp.minimum(1.0, bound / jnp.sqrt(norm_sq + 1e-06))
    total = part_in[0].astype(F32) * clip[:, 0:1]
    for o in range(1, images):
        total = total + part_in[o].astype(F32) * clip[:, o : o + 1]
    sum_ref[...] = total
    pltpu.make_async_copy(norm_all, norm_all, norm_sem.at[0]).wait()


def local(draws, images, features, cotangent, time_index, mod_table, weight):
    pixels, in_width = features.shape[2:]
    out_width = cotangent.shape[3]
    table_rows = mod_table.shape[0]
    stratum = table_rows - (draws - 1) * table_rows // draws
    window = (stratum + 14) // 8
    piece = in_width // draws
    each = piece // images
    hops = draws // 4
    dma = pltpu.SemaphoreType.DMA
    return pl.pallas_call(
        functools.partial(kernel, draws, images, table_rows, window),
        out_shape=(
            pltpu.VMEM((each, out_width), F32),
            pltpu.VMEM(features.shape, BF16),
        ),
        in_specs=[pl.BlockSpec(memory_space=pltpu.HBM)] * 5,
        out_specs=(
            pl.BlockSpec(memory_space=pltpu.VMEM),
            pl.BlockSpec(memory_space=pltpu.VMEM),
        ),
        scratch_shapes=[
            pltpu.VMEM((pixels, in_width), BF16),
            pltpu.VMEM((pixels, out_width), BF16),
            pltpu.VMEM((1, 1), jnp.int32),
            pltpu.VMEM((window, 8, in_width), BF16),
            pltpu.VMEM((in_width, out_width), BF16),
            pltpu.VMEM((1, in_width), F32),
            pltpu.VMEM((pixels, out_width), BF16),
            pltpu.VMEM((in_width, out_width), F32),
            pltpu.VMEM((draws // 2, piece, out_width), BF16),
            pltpu.VMEM((draws // 2, piece, out_width), BF16),
            pltpu.VMEM((2, hops, piece, out_width), BF16),
            pltpu.VMEM((2, hops, piece, out_width), BF16),
            pltpu.VMEM((2, 2, hops, piece, out_width), BF16),
            pltpu.VMEM((2, 2, hops, piece, out_width), BF16),
            pltpu.VMEM((2, piece, out_width), F32),
            pltpu.VMEM((piece, out_width), BF16),
            pltpu.VMEM((piece, out_width), BF16),
            pltpu.VMEM((1, LANES), F32),
            pltpu.VMEM((images, 1, LANES), F32),
            pltpu.VMEM((1, LANES), F32),
            pltpu.VMEM((draws, 1, LANES), F32),
            pltpu.VMEM((images, each, out_width), BF16),
            pltpu.VMEM((images, each, out_width), BF16),
            dma((5,)),
            dma((draws // 2,)),
            dma((draws // 2,)),
            dma((2, hops)),
            dma((2, hops)),
            dma((2, 2, hops)),
            dma((2, 2, hops)),
            dma((2,)),
            dma((2,)),
            dma((2,)),
            dma((2,)),
        ],
        compiler_params=pltpu.CompilerParams(
            collective_id=0, has_side_effects=True, vmem_limit_bytes=60 * 2**20
        ),
        cost_estimate=pl.CostEstimate(
            flops=4 * pixels * in_width * out_width,
            bytes_accessed=2 * (2 * pixels * in_width + pixels * out_width + in_width * out_width),
            transcendentals=2 * pixels * in_width,
        ),
    )(
        features,
        cotangent,
        time_index,
        mod_table.reshape(table_rows // 8, 8, in_width),
        weight,
    )


def solution(mesh):
    in_specs = (
        P("img", "draw", None, None),
        P("img", "draw", None, None),
        P("img", "draw"),
        P(),
        P(),
    )
    out_specs = (P(("draw", "img"), None), P("img", "draw", None, None))
    body = functools.partial(local, mesh.shape["draw"], mesh.shape["img"])
    return jax.shard_map(body, mesh=mesh, in_specs=in_specs, out_specs=out_specs, check_vma=False)
```

time: 56.2 us -> 51.9 us (0.923)
  Pallas kernels: 51.5 us -> 49.1 us
  local copies, waits for them, and re-layouts: 3.15 us -> 1.39 us
    pallas_call x1, Pallas kernels: 51.5 us -> 49.1 us  [local(): pl.pallas_call(functools.partial(kernel, draws, images, table_rows, windo...]
    unnamed x2, local copies, waits for them, and re-layouts: 3.15 us -> 1.39 us
where the time goes in v3:
time: 51.9 us; the launch traced here: 51.7 us
  Pallas kernels  49.1 us (95%)
  local copies, waits for them, and re-layouts  1.39 us (3%)
  between operations  1.28 us (2%)
    pallas_call x1, Pallas kernels, local(): pl.pallas_call(functools.partial(kernel, draws, images, table_rows, windo...  49.1 us
    unnamed x2, local copies, waits for them, and re-layouts  1.39 us

profile of v3, /device:TPU:1, one launch (start us, length us, event | category | flops | bytes accessed | tf_op | source)
XLA Modules:
  0.0 51.7 jit_solution(15023185207575218976)
XLA Ops:
  1.3 49.1 %shard_map.68 = (f32[2,640]{1,0:T(2,128)S(1)}, bf16[1,1,256,1024]{3,2,1,0:T(8,128)(2,1)S(1)}) custom-call(bf16[1,1,256,1024]{3,2,1,0:T(8,128)(2,1)} %feat_hbm.1, bf16[1,1,256,640]{3,2,1,0:T(8,128)(2,1)} %cot_hbm.1, s32[1,1]{1,0:T(1,128)S(6)} %copy.11.time_hbm, bf16[125,8,1024]{2,1,0:T(8,128)(2,1)} %bitcast.1, bf16[1024,640]{1,0:T(8,128)(2,1)} %weight_hbm.1), custom_call_target="tpu_custom_call" | custom-call | flops 671088640 | bytes 2686976 | tf_op jit(solution)/shard_map/pallas_call | solution.py:322
  50.4 0.6 %copy.9 = f32[2,640]{1,0:T(2,128)} copy(f32[2,640]{1,0:T(2,128)S(1)} %get-tuple-element.2) | data formatting | bytes 10240
  51.0 0.8 %copy.10 = bf16[1,1,256,1024]{3,2,1,0:T(8,128)(2,1)} copy(bf16[1,1,256,1024]{3,2,1,0:T(8,128)(2,1)S(1)} %get-tuple-element.3) | data formatting | bytes 1048576

commit v4 on v3

v4 whole, which is shorter than its diff:
```python
import functools
import math

import jax
import jax.numpy as jnp
from jax import lax
from jax.experimental import pallas as pl
from jax.experimental.pallas import tpu as pltpu
from jax.sharding import PartitionSpec as P

MESH = pl.DeviceIdType.MESH
F32 = jnp.float32
BF16 = jnp.bfloat16
LANES = 128
ROUNDS = 4
NEAR = {2: 1, 1: 0}
FAR = {8: 6, 7: 6, 6: 3, 5: 4, 4: 3, 3: 0}


def sigmoid(v):
    return 1.0 / (1.0 + jnp.exp(-v))


def tree_levels(tree):
    level = {}
    for node in sorted(tree, reverse=True):
        level[node] = max([level[c] + 1 for c in tree if tree[c] == node], default=0)
    for node in sorted(tree):
        if tree[node] in tree:
            level[node] = max(level[node], level[tree[node]] - 1)
    return level


def kernel(
    draws, images, table_rows, window,
    feat_hbm, cot_hbm, time_hbm, table_hbm, weight_hbm,
    sum_ref, gi_ref,
    feat, cot, when, rows, weight, gain, weighted, grad,
    first_out, first_in, xsend, xrecv, zsend, zrecv, root_in,
    share_out, share_in, norm_out, norm_in, part_out, part_in,
    load_sem, first_send, first_recv, xsend_sem, xrecv_sem, zsend_sem, zrecv_sem,
    root_recv, share_sem, norm_sem, part_sem, relay,
):
    in_width = feat.shape[1]
    out_width = cot.shape[1]
    ring = draws // 2
    half_rows = in_width // 2
    piece = in_width // draws
    each = piece // images
    k = lax.axis_index("draw")
    image = lax.axis_index("img")
    high = lax.div(k, ring)
    z = lax.rem(k, ring)

    def around(offset):
        return lax.rem(z + (offset + ring), ring)

    def at_z(offset):
        return {"draw": high * ring + around(offset)}

    partner = {"draw": (1 - high) * ring + z}

    first_row = lax.div(k * table_rows, draws)
    first_block = jnp.minimum(lax.div(first_row, 8), table_rows // 8 - window)
    loads = [
        pltpu.make_async_copy(time_hbm, when, load_sem.at[0]),
        pltpu.make_async_copy(table_hbm.at[pl.ds(first_block, window)], rows, load_sem.at[1]),
        pltpu.make_async_copy(cot_hbm.at[0, 0], cot, load_sem.at[2]),
        pltpu.make_async_copy(feat_hbm.at[0, 0], feat, load_sem.at[3]),
        pltpu.make_async_copy(weight_hbm, weight, load_sem.at[4]),
    ]
    for load in loads:
        load.start()

    apart = ring // 2
    turned = 1 - lax.div(around(ring // 4), apart)

    for way in range(2):
        xrecv[way, apart - 1] = jnp.zeros(xrecv.shape[2:], BF16)

    y, bits = lax.div(image, 4), lax.rem(image, 4)
    bit_x, bit_core = lax.div(bits, 2), lax.rem(bits, 2)
    planes = images // 4
    neighbours = [
        at_z(1),
        at_z(-1),
        {"img": lax.rem(y + 1, planes) * 4 + bits},
        {"img": lax.rem(y + planes - 1, planes) * 4 + bits},
        {"img": image + 2 - 4 * bit_x},
        {"img": image + 1 - 2 * bit_core},
    ]
    barrier = pltpu.get_barrier_semaphore()
    for device in [partner] + neighbours:
        pl.semaphore_signal(barrier, inc=1, device_id=device, device_id_type=MESH)

    def tell(turn):
        for device in neighbours:
            pl.semaphore_signal(relay.at[turn], inc=1, device_id=device, device_id_type=MESH)

    def hear(turn):
        pl.semaphore_wait(relay.at[turn], len(neighbours))

    for load in loads[:3]:
        load.wait()
    step = when[...]
    index = (
        lax.broadcasted_iota(jnp.int32, (window, 8, 1), 0) * 8
        + lax.broadcasted_iota(jnp.int32, (window, 8, 1), 1)
        + first_block * 8
    )
    chosen = jnp.where(index == step.reshape(1, 1, 1), rows[...].astype(F32), 0.0)
    gain[...] = 1.0 + jnp.sum(jnp.sum(chosen, axis=0), axis=0, keepdims=True)
    loss_scale = 1.0 + 2.0 * step.astype(F32) / (table_rows - 1)
    weighted[...] = (cot[...].astype(F32) * loss_scale).astype(BF16)
    loads[3].wait()

    def local_gradient(half):
        for n in range(half_rows // LANES):
            at = pl.ds(pl.multiple_of(half * half_rows + n * LANES, LANES), LANES)
            pre_act = feat[:, at].astype(F32) * gain[:, at]
            acts = (pre_act * sigmoid(pre_act)).astype(BF16)
            grad[at, :] = lax.dot_general(
                acts, weighted[...], (((0,), (0,)), ((), ())), preferred_element_type=F32
            )

    local_gradient(1 - high)
    pl.semaphore_wait(barrier, len(neighbours) + 1)
    tell(0)

    def own(half, offset):
        start = half * half_rows + around(offset) * piece
        return grad[pl.ds(pl.multiple_of(start, piece), piece), :]

    def first_copy(n):
        return pltpu.make_async_remote_copy(
            src_ref=first_out.at[n],
            dst_ref=first_in.at[n],
            send_sem=first_send.at[n],
            recv_sem=first_recv.at[n],
            device_id=partner,
            device_id_type=MESH,
        )

    def near_copy(half, way, node, hop):
        return pltpu.make_async_remote_copy(
            src_ref=zsend.at[half, way, node - 1],
            dst_ref=zrecv.at[half, way, node - 1],
            send_sem=zsend_sem.at[half, way, node - 1],
            recv_sem=zrecv_sem.at[half, way, node - 1],
            device_id=at_z(hop * (1 - 2 * way)),
            device_id_type=MESH,
        )

    def root_copy(half, way, hop, column):
        return pltpu.make_async_remote_copy(
            src_ref=zsend.at[half, way, hop - 1],
            dst_ref=root_in.at[column, way],
            send_sem=zsend_sem.at[half, way, hop - 1],
            recv_sem=root_recv.at[column, way],
            device_id={"draw": half * ring + around(hop * (1 - 2 * way))},
            device_id_type=MESH,
        )

    def far_copy(way, node, hop):
        part = pl.ds(0, piece)
        if node == apart:
            part = pl.ds(pl.multiple_of(way * (piece // 2), piece // 2), piece // 2)
        return pltpu.make_async_remote_copy(
            src_ref=xsend.at[way, node - 1, part],
            dst_ref=xrecv.at[way, node - 1, part],
            send_sem=xsend_sem.at[way, node - 1],
            recv_sem=xrecv_sem.at[way, node - 1],
            device_id=at_z(hop * (1 - 2 * way)),
            device_id_type=MESH,
        )

    def children(tree, node):
        return [c for c in tree if tree[c] == node]

    def near_sum(half, way, node, term):
        for child in children(NEAR, node):
            near_copy(half, way, child, child - node).wait_recv()
            term = term + zrecv[half, way, child - 1].astype(F32)
        return term

    def far_sum(way, node, term):
        for child in children(FAR, node):
            far_copy(way, child, child - node).wait_recv()
            term = term + xrecv[way, child - 1].astype(F32)
        return term

    def grad_input_block(block):
        at = pl.ds(block * LANES, LANES)
        back = lax.dot_general(
            weighted[...], weight[at, :], (((1,), (1,)), ((), ())), preferred_element_type=F32
        )
        scale = gain[:, at]
        pre_act = feat[:, at].astype(F32) * scale
        gate = sigmoid(pre_act)
        gi_ref[0, 0, :, at] = (back * gate * (1.0 + pre_act * (1.0 - gate)) * scale).astype(BF16)

    jobs = []
    for way in range(2):
        for node, level in tree_levels(NEAR).items():
            jobs += [(level, 0, -node, way, half) for half in range(2)]
        for node, level in tree_levels(FAR).items():
            jobs.append((level, 1, -node, way, 0))
    jobs.sort()
    sent = []
    known = 1
    offsets = [0]
    for _, kind, minus, way, _ in reversed(jobs):
        offset = (-minus if way == 0 else minus) % ring
        if kind == 1 and offset not in offsets:
            offsets.insert(0, offset)
    for offset in offsets:
        first_out[offset] = own(1 - high, offset).astype(BF16)
        sent.append(first_copy(offset))
        sent[-1].start()
    local_gradient(high)

    def greet_more(known):
        hear(known - 1)
        if known < ROUNDS:
            tell(known)
        return known + 1

    for at, (level, kind, minus, first, half) in enumerate(jobs):
        node = -minus
        hop = node - (FAR if kind else NEAR)[node]
        way = first + turned - 2 * first * turned
        offset = node * (1 - 2 * way)
        while known < (2 if kind == 0 and node == hop else hop):
            known = greet_more(known)
        if kind == 0:
            term = near_sum(half, way, node, own(half, offset))
            zsend[half, way, node - 1] = term.astype(BF16)
            if node == hop:
                copy = root_copy(half, way, hop, high)
            else:
                copy = near_copy(half, way, node, hop)
        else:
            slot = lax.rem(offset + ring, ring)
            if node < apart or first == 0:
                first_copy(slot).wait_recv()
            term = own(high, offset) + first_in[slot].astype(F32)
            xsend[way, node - 1] = far_sum(way, node, term).astype(BF16)
            copy = far_copy(way, node, hop)
        copy.start()
        sent.append(copy)
        if at + 1 == len(jobs) or jobs[at + 1][0] > level:
            if known < ROUNDS + 1:
                known = greet_more(known)

    while known < ROUNDS + 1:
        known = greet_more(known)

    mine = own(high, 0)
    first_copy(0).wait_recv()
    mine = mine + first_in[0].astype(F32)
    for way in range(2):
        (hop,) = children(NEAR, 0)
        for column in range(2):
            root_copy(0, way, hop, column).wait_recv()
            mine = mine + root_in[column, way].astype(F32)
    for way in range(2):
        mine = far_sum(way, 0, mine)
    mine = mine * (1.0 / draws)

    def finish():
        for copy in sent:
            copy.wait_send()


    square = mine * mine
    tile = square[:, 0:LANES]
    for c in range(1, out_width // LANES):
        tile = tile + square[:, c * LANES : (c + 1) * LANES]
    share_out[...] = jnp.sum(tile, axis=0, keepdims=True)

    def share_start(o, _):
        pltpu.make_async_remote_copy(
            src_ref=share_out,
            dst_ref=share_in.at[o],
            send_sem=share_sem.at[0],
            recv_sem=share_sem.at[1],
            device_id=at_z(o),
            device_id_type=MESH,
        ).start()
        return 0

    lax.fori_loop(1, ring, share_start, 0)
    for j in range(images):
        part_out[j] = mine[j * each : (j + 1) * each, :].astype(BF16)

    def part_start(o, _):
        to = lax.rem(image + o, images)
        pltpu.make_async_remote_copy(
            src_ref=part_out.at[to],
            dst_ref=part_in.at[o],
            send_sem=part_sem.at[0],
            recv_sem=part_sem.at[1],
            device_id={"img": to},
            device_id_type=MESH,
        ).start()
        return 0

    lax.fori_loop(1, images, part_start, 0)
    share_in[0] = share_out[...]
    part_in[0] = part_out[image]

    loads[4].wait()
    for block in range(in_width // LANES):
        grad_input_block(block)
    finish()
    part_all = part_in.at[pl.ds(1, images - 1)]
    pltpu.make_async_copy(part_all, part_all, part_sem.at[1]).wait()
    pltpu.make_async_copy(part_all, part_all, part_sem.at[0]).wait()
    share_all = share_in.at[pl.ds(1, ring - 1)]
    pltpu.make_async_copy(share_all, share_all, share_sem.at[1]).wait()

    norm_out[...] = jnp.sum(share_in[...], axis=0)

    def norm_copy(o, to):
        return pltpu.make_async_remote_copy(
            src_ref=norm_out,
            dst_ref=norm_in.at[o],
            send_sem=norm_sem.at[0],
            recv_sem=norm_sem.at[1],
            device_id=to,
            device_id_type=MESH,
        )

    def norm_start(o, _):
        to = lax.rem(image + o, images)
        norm_copy(images + o, {"draw": partner["draw"], "img": to}).start()
        norm_copy(o, {"img": to}).start()
        return 0

    lax.fori_loop(1, images, norm_start, 0)
    norm_copy(images, partner).start()
    norm_in[0] = norm_out[...]
    norm_all = norm_in.at[pl.ds(1, 2 * images - 1)]
    pltpu.make_async_copy(norm_all, norm_all, norm_sem.at[1]).wait()
    norm_sq = jnp.sum(norm_in[0:images] + norm_in[images:], axis=2, keepdims=True)
    bound = 0.3 * math.sqrt(in_width * out_width)
    clip = jnp.minimum(1.0, bound / jnp.sqrt(norm_sq + 1e-06))
    sum_ref[...] = jnp.sum(part_in[...].astype(F32) * clip, axis=0)
    pltpu.make_async_copy(share_all, share_all, share_sem.at[0]).wait()
    pltpu.make_async_copy(norm_all, norm_all, norm_sem.at[0]).wait()


def local(draws, images, features, cotangent, time_index, mod_table, weight):
    pixels, in_width = features.shape[2:]
    out_width = cotangent.shape[3]
    table_rows = mod_table.shape[0]
    stratum = table_rows - (draws - 1) * table_rows // draws
    window = (stratum + 14) // 8
    piece = in_width // draws
    each = piece // images
    hops = draws // 4
    dma = pltpu.SemaphoreType.DMA
    return pl.pallas_call(
        functools.partial(kernel, draws, images, table_rows, window),
        out_shape=(
            pltpu.VMEM((each, out_width), F32),
            pltpu.VMEM(features.shape, BF16),
        ),
        in_specs=[pl.BlockSpec(memory_space=pltpu.HBM)] * 5,
        out_specs=(
            pl.BlockSpec(memory_space=pltpu.VMEM),
            pl.BlockSpec(memory_space=pltpu.VMEM),
        ),
        scratch_shapes=[
            pltpu.VMEM((pixels, in_width), BF16),
            pltpu.VMEM((pixels, out_width), BF16),
            pltpu.VMEM((1, 1), jnp.int32),
            pltpu.VMEM((window, 8, in_width), BF16),
            pltpu.VMEM((in_width, out_width), BF16),
            pltpu.VMEM((1, in_width), F32),
            pltpu.VMEM((pixels, out_width), BF16),
            pltpu.VMEM((in_width, out_width), F32),
            pltpu.VMEM((draws // 2, piece, out_width), BF16),
            pltpu.VMEM((draws // 2, piece, out_width), BF16),
            pltpu.VMEM((2, hops, piece, out_width), BF16),
            pltpu.VMEM((2, hops, piece, out_width), BF16),
            pltpu.VMEM((2, 2, hops, piece, out_width), BF16),
            pltpu.VMEM((2, 2, hops, piece, out_width), BF16),
            pltpu.VMEM((2, 2, piece, out_width), BF16),
            pltpu.VMEM((1, LANES), F32),
            pltpu.VMEM((draws // 2, 1, LANES), F32),
            pltpu.VMEM((1, LANES), F32),
            pltpu.VMEM((2 * images, 1, LANES), F32),
            pltpu.VMEM((images, each, out_width), BF16),
            pltpu.VMEM((images, each, out_width), BF16),
            dma((5,)),
            dma((draws // 2,)),
            dma((draws // 2,)),
            dma((2, hops)),
            dma((2, hops)),
            dma((2, 2, hops)),
            dma((2, 2, hops)),
            dma((2, 2)),
            dma((2,)),
            dma((2,)),
            dma((2,)),
            pltpu.SemaphoreType.REGULAR((ROUNDS,)),
        ],
        compiler_params=pltpu.CompilerParams(
            collective_id=0, has_side_effects=True, vmem_limit_bytes=60 * 2**20
        ),
        cost_estimate=pl.CostEstimate(
            flops=4 * pixels * in_width * out_width,
            bytes_accessed=2 * (2 * pixels * in_width + pixels * out_width + in_width * out_width),
            transcendentals=2 * pixels * in_width,
        ),
    )(
        features,
        cotangent,
        time_index,
        mod_table.reshape(table_rows // 8, 8, in_width),
        weight,
    )


def solution(mesh):
    in_specs = (
        P("img", "draw", None, None),
        P("img", "draw", None, None),
        P("img", "draw"),
        P(),
        P(),
    )
    out_specs = (P(("draw", "img"), None), P("img", "draw", None, None))
    body = functools.partial(local, mesh.shape["draw"], mesh.shape["img"])
    return jax.shard_map(body, mesh=mesh, in_specs=in_specs, out_specs=out_specs, check_vma=False)
```

time: 51.9 us -> 50.8 us (0.979)
  Pallas kernels: 49.1 us -> 48 us
    pallas_call x1, Pallas kernels: 49.1 us -> 48 us  [local(): pl.pallas_call(functools.partial(kernel, draws, images, table_rows, windo...]
where the time goes in v4:
time: 50.8 us; the launch traced here: 50.7 us
  Pallas kernels  48 us (94%)
  local copies, waits for them, and re-layouts  1.39 us (3%)
  between operations  1.28 us (3%)
    pallas_call x1, Pallas kernels, local(): pl.pallas_call(functools.partial(kernel, draws, images, table_rows, windo...  48 us
    unnamed x2, local copies, waits for them, and re-layouts  1.39 us

profile of v4, /device:TPU:1, one launch (start us, length us, event | category | flops | bytes accessed | tf_op | source)
XLA Modules:
  0.0 50.7 jit_solution(11568550562564132354)
XLA Ops:
  1.3 48.0 %shard_map.68 = (f32[2,640]{1,0:T(2,128)S(1)}, bf16[1,1,256,1024]{3,2,1,0:T(8,128)(2,1)S(1)}) custom-call(bf16[1,1,256,1024]{3,2,1,0:T(8,128)(2,1)} %feat_hbm.1, bf16[1,1,256,640]{3,2,1,0:T(8,128)(2,1)} %cot_hbm.1, s32[1,1]{1,0:T(1,128)S(6)} %copy.11.time_hbm, bf16[125,8,1024]{2,1,0:T(8,128)(2,1)} %bitcast.1, bf16[1024,640]{1,0:T(8,128)(2,1)} %weight_hbm.1), custom_call_target="tpu_custom_call" | custom-call | flops 671088640 | bytes 2686976 | tf_op jit(solution)/shard_map/pallas_call | solution.py:363
  49.3 0.6 %copy.9 = f32[2,640]{1,0:T(2,128)} copy(f32[2,640]{1,0:T(2,128)S(1)} %get-tuple-element.2) | data formatting | bytes 10240
  49.9 0.8 %copy.10 = bf16[1,1,256,1024]{3,2,1,0:T(8,128)(2,1)} copy(bf16[1,1,256,1024]{3,2,1,0:T(8,128)(2,1)S(1)} %get-tuple-element.3) | data formatting | bytes 1048576

commit v5 on v4

--- a/solution.py
+++ b/solution.py
@@ -69,7 +69,7 @@
         pltpu.make_async_copy(feat_hbm.at[0, 0], feat, load_sem.at[3]),
         pltpu.make_async_copy(weight_hbm, weight, load_sem.at[4]),
     ]
-    for load in loads:
+    for load in loads[:4]:
         load.start()
 
     apart = ring // 2
@@ -218,6 +218,7 @@
         sent.append(first_copy(offset))
         sent[-1].start()
     local_gradient(high)
+    loads[4].start()
 
     def greet_more(known):
         hear(known - 1)
@@ -248,9 +249,6 @@
             copy = far_copy(way, node, hop)
         copy.start()
         sent.append(copy)
-        if at + 1 == len(jobs) or jobs[at + 1][0] > level:
-            if known < ROUNDS + 1:
-                known = greet_more(known)
 
     while known < ROUNDS + 1:
         known = greet_more(known)

time: 50.8 us -> 50.6 us (level)
  no operation moved by 1% of the time
where the time goes in v5:
time: 50.6 us; the launch traced here: 50.4 us
  Pallas kernels  47.8 us (94%)
  local copies, waits for them, and re-layouts  1.39 us (3%)
  between operations  1.28 us (3%)
    pallas_call x1, Pallas kernels, local(): pl.pallas_call(functools.partial(kernel, draws, images, table_rows, windo...  47.8 us
    unnamed x2, local copies, waits for them, and re-layouts  1.39 us

profile of v5, /device:TPU:1, one launch (start us, length us, event | category | flops | bytes accessed | tf_op | source)
XLA Modules:
  0.0 50.4 jit_solution(5475029292618348076)
XLA Ops:
  1.3 47.8 %shard_map.68 = (f32[2,640]{1,0:T(2,128)S(1)}, bf16[1,1,256,1024]{3,2,1,0:T(8,128)(2,1)S(1)}) custom-call(bf16[1,1,256,1024]{3,2,1,0:T(8,128)(2,1)} %feat_hbm.1, bf16[1,1,256,640]{3,2,1,0:T(8,128)(2,1)} %cot_hbm.1, s32[1,1]{1,0:T(1,128)S(6)} %copy.11.time_hbm, bf16[125,8,1024]{2,1,0:T(8,128)(2,1)} %bitcast.1, bf16[1024,640]{1,0:T(8,128)(2,1)} %weight_hbm.1), custom_call_target="tpu_custom_call" | custom-call | flops 671088640 | bytes 2686976 | tf_op jit(solution)/shard_map/pallas_call | solution.py:361
  49.0 0.6 %copy.9 = f32[2,640]{1,0:T(2,128)} copy(f32[2,640]{1,0:T(2,128)S(1)} %get-tuple-element.2) | data formatting | bytes 10240
  49.6 0.8 %copy.10 = bf16[1,1,256,1024]{3,2,1,0:T(8,128)(2,1)} copy(bf16[1,1,256,1024]{3,2,1,0:T(8,128)(2,1)S(1)} %get-tuple-element.3) | data formatting | bytes 1048576
